TPU v7x, 128 devices: a whole 4x4x4 slice. The times are simulated.
128 devices in a mesh: row: 16 (over y, z_lo, core), col: 8 (over x, z_hi).
Axes of the slice: x: 4, y: 4, z: 4 (z_hi: 2, z_lo: 2; z = z_hi * 2 + z_lo), core: 2. Of those that a mesh axis runs over, the one named last changes fastest.
Arguments:
- tokens: bfloat16 [512, 16384], P('col', 'row'), may hold values from -6 to 6
- weight: bfloat16 [16384, 26624], P('row', 'col'), may hold values from -0.046875 to 0.046875
- adapter_down_matrix: bfloat16 [16384, 64], P('row'), may hold values from -0.046875 to 0.046875
- adapter_up_matrix: bfloat16 [64, 26624], P(None, 'col'), may hold values from -0.75 to 0.75
- grad_out: bfloat16 [512, 26624], P('row', 'col'), may hold values from -6 to 6
- tile_list: int32 [16, 8, 156], P('row', 'col'), may hold values from 0 to 208, as said below
Outputs:
- projected: bfloat16 [512, 26624], P('row', 'col')
- grad_tokens: bfloat16 [512, 16384], P('col', 'row')
- grad_weight: bfloat16 [16384, 26624], P('row', 'col')
Inputs may be any that keep to these rules, and one draw needn't show every extreme that they name: Each list tile_list[r, c] holds the distinct kept tile numbers of block (r, c) in increasing order, followed by the filler 208; a block keeps between 52 and 156 tiles.
All inputs are finite; a program needn't handle non-finite values.
Results may differ from a plain program's by a relative error of at most 0.001.
Values may be sent and summed in bfloat16 or wider, within the bound.
A program may use at most 128 MiB of HBM per device.

v0:
```python
import math

import jax
import jax.numpy as jnp
from jax import lax
from jax.sharding import PartitionSpec as P

TILE_SIDE = 128
TOKENS = 512


def body(tokens, weight, adapter_down_matrix, adapter_up_matrix, grad_out, tile_list):
    side = TILE_SIDE
    grad_scale = 1.0 / math.sqrt(TOKENS)
    rows, cols = weight.shape
    nrow = rows // side
    ncol = cols // side
    ntile = nrow * ncol
    listed = tile_list.reshape(-1)
    up_float = adapter_up_matrix.astype(jnp.float32)
    down_matrix_float = adapter_down_matrix.astype(jnp.float32)
    x_all = lax.all_gather(tokens, "col", axis=0, tiled=True)
    low_part = jnp.dot(x_all, adapter_down_matrix, preferred_element_type=jnp.float32)
    flags = jnp.any(listed[:, None] == jnp.arange(ntile, dtype=jnp.int32)[None, :], axis=0)
    grid = flags.reshape(nrow, ncol)
    mask = jnp.repeat(jnp.repeat(grid, side, axis=0), side, axis=1).astype(jnp.bfloat16)
    masked = weight * mask
    out_part = jnp.dot(x_all, masked, preferred_element_type=jnp.float32)
    out_sum = lax.psum_scatter(out_part, "row", scatter_dimension=0, tiled=True)
    low = lax.psum(low_part, "row")
    share = out_sum.shape[0]
    mine = lax.dynamic_slice_in_dim(low, lax.axis_index("row") * share, share, 0)
    out_sum = out_sum + jnp.dot(mine, up_float, precision=lax.Precision.HIGHEST)
    projected = out_sum.astype(jnp.bfloat16)
    dy_all = lax.all_gather(grad_out, "row", axis=0, tiled=True)
    gradient_lowrank_partial = lax.dot_general(
        dy_all, adapter_up_matrix, (((1,), (1,)), ((), ())), preferred_element_type=jnp.float32
    )
    in_part = lax.dot_general(
        dy_all, masked, (((1,), (1,)), ((), ())), preferred_element_type=jnp.float32
    )
    outer = lax.dot_general(
        x_all, dy_all, (((0,), (0,)), ((), ())), preferred_element_type=jnp.float32
    )
    grad_weight = (outer * mask * grad_scale).astype(jnp.bfloat16)
    in_sum = lax.psum_scatter(in_part, "col", scatter_dimension=0, tiled=True)
    grad_low = lax.psum(gradient_lowrank_partial, "col")
    share_in = in_sum.shape[0]
    mine_in = lax.dynamic_slice_in_dim(grad_low, lax.axis_index("col") * share_in, share_in, 0)
    in_sum = in_sum + jnp.dot(mine_in, down_matrix_float.T, precision=lax.Precision.HIGHEST)
    grad_tokens = in_sum.astype(jnp.bfloat16)
    return (projected, grad_tokens, grad_weight)


def solution(mesh):
    return jax.shard_map(
        body,
        mesh=mesh,
        in_specs=(
            P("col", "row"),
            P("row", "col"),
            P("row", None),
            P(None, "col"),
            P("row", "col"),
            P("row", "col", None),
        ),
        out_specs=(P("row", "col"), P("col", "row"), P("row", "col")),
        check_vma=False,
    )
```

profile of v0, /device:TPU:0, one launch (start us, length us, event | category | flops | bytes accessed | tf_op | source)
XLA Modules:
  0.0 470.8 jit_solution(1958629764590466853)
XLA Ops:
  7.2 0.7 all-gather.5.cloned.1.call-update
  8.0 0.7 all-gather.3.cloned.1.call-update
  8.7 9.9 %copy.32 = bf16[1024,3328]{0,1:T(8,128)(2,1)} copy(bf16[1024,3328]{1,0:T(8,128)(2,1)} %param.7) | data formatting | bytes 13631488 | tf_op args[1]
  18.7 0.1 fusion.2
  18.9 0.1 copy.31
  19.1 6.5 %bitcast_select_fusion = bf16[1024,3328]{0,1:T(8,128)(2,1)} fusion(bf16[1024,3328]{0,1:T(8,128)(2,1)} %copy.32, pred[1024,26]{0,1:T(8,128)(4,1)S(1)} %bitcast.28), kind=kLoop, calls=%fused_computation.1 | loop fusion | flops 3407872 | bytes 13658112 | tf_op jit(solution)/shard_map/mul | solution.py:27
  25.6 23.0 %all-gather.5.cloned.1.call-done = bf16[512,3328]{1,0:T(8,128)(2,1)} async-done(((bf16[32,3328]{1,0:T(8,128)(2,1)}), bf16[512,3328]{1,0:T(8,128)(2,1)}) %all-gather.5.cloned.1.call-update) | async-done | bytes 3407888 | tf_op jit(solution)/shard_map/all_gather | solution.py:35
  48.6 3.7 fusion.8
  52.4 7.0 %convolution_bitcast_fusion.1 = f32[512,1024]{0,1:T(8,128)S(1)} fusion(bf16[1024,3328]{0,1:T(8,128)(2,1)} %bitcast_select_fusion, bf16[512,3328]{1,0:T(8,128)(2,1)} %all-gather.5.cloned.1.call-done), kind=kOutput, calls=%fused_computation.5 | convolution fusion | flops 3489660928 | bytes 12320768 | tf_op jit(solution)/shard_map/dot_general | solution.py:39
  59.4 1.8 copy.38
  61.3 37.1 %all-gather.3.cloned.1.call-done = bf16[512,1024]{1,0:T(8,128)(2,1)} async-done(((bf16[64,1024]{1,0:T(8,128)(2,1)}), bf16[512,1024]{1,0:T(8,128)(2,1)}) %all-gather.3.cloned.1.call-update) | async-done | bytes 1048592 | tf_op jit(solution)/shard_map/all_gather | solution.py:22
  98.4 2.4 fusion.7
  100.7 0.2 reduce-scatter.7.cloned.1.call-start
  101.0 9.8 %convolution_bitcast_fusion = f32[512,3328]{0,1:T(8,128)} fusion(bf16[1024,3328]{0,1:T(8,128)(2,1)} %bitcast_select_fusion, bf16[512,1024]{1,0:T(8,128)(2,1)} %all-gather.3.cloned.1.call-done), kind=kOutput, calls=%fused_computation.2 | convolution fusion | flops 3489660928 | bytes 14680064 | tf_op jit(solution)/shard_map/dot_general | solution.py:28
  110.7 7.7 %copy.36 = f32[512,3328]{1,0:T(8,128)} copy(f32[512,3328]{0,1:T(8,128)} %convolution_bitcast_fusion) | data formatting | bytes 13631488
  118.5 0.9 broadcast_in_dim.8
  119.4 5.4 %copy.35 = pred[1024,3328]{1,0:T(32,128)(4,1)} copy(pred[1024,3328]{0,1:T(32,128)(4,1)S(1)} %bitcast.27) | data formatting | bytes 6815744 | tf_op jit(solution)/shard_map/reshape | solution.py:26
  124.8 8.9 %multiply_convert_fusion = bf16[1024,3328]{1,0:T(8,128)(2,1)} fusion(bf16[512,1024]{1,0:T(8,128)(2,1)S(1)} %copy-done.1, bf16[512,3328]{1,0:T(8,128)(2,1)} %all-gather.5.cloned.1.call-done, pred[1024,3328]{1,0:T(32,128)(4,1)} %copy.35), kind=kOutput, calls=%fused_computation | convolution fusion | flops 3506700288 | bytes 14680064 | tf_op jit(solution)/shard_map/dot_general | solution.py:42
  133.7 50.2 %all-reduce.5.cloned.1.call-done = f32[512,64]{1,0:T(8,128)} async-done(((f32[512,64]{1,0:T(8,128)}), f32[512,64]{1,0:T(8,128)}) %all-reduce.5.cloned.1.call-update) | async-done | bytes 131088 | tf_op jit(solution)/shard_map/psum | solution.py:47
  183.8 77.2 %reduce-scatter.9.cloned.1.call-done = f32[64,1024]{1,0:T(8,128)} async-done(((f32[512,1024]{1,0:T(8,128)}), f32[64,1024]{1,0:T(8,128)}) %reduce-scatter.9.cloned.1.call-update) | async-done | bytes 262160 | tf_op jit(solution)/shard_map/reduce_scatter | solution.py:46
  261.0 1.9 fusion.1
  262.9 115.5 %all-reduce.3.cloned.1.call-done = f32[512,64]{1,0:T(8,128)} async-done(((f32[512,64]{1,0:T(8,128)}), f32[512,64]{1,0:T(8,128)}) %all-reduce.3.cloned.1.call-update) | async-done | bytes 131088 | tf_op jit(solution)/shard_map/psum | solution.py:30
  378.4 83.5 %reduce-scatter.7.cloned.1.call-done = f32[32,3328]{1,0:T(8,128)} async-done(((f32[512,3328]{1,0:T(8,128)}), f32[32,3328]{1,0:T(8,128)}) %reduce-scatter.7.cloned.1.call-update) | async-done | bytes 426000 | tf_op jit(solution)/shard_map/reduce_scatter | solution.py:29
  461.9 2.0 fusion
  (21 shorter events, 0.5 us)
Async XLA Ops:
  7.2 41.5 %copy-start = (bf16[64,3328]{1,0:T(8,128)(2,1)S(1)}, bf16[64,3328]{1,0:T(8,128)(2,1)}, u32[]{:S(2)}) copy-start(bf16[64,3328]{1,0:T(8,128)(2,1)} %param.9) | copy-start | bytes 1277956
  7.2 41.4 %all-gather.5.cloned.1.call-start = ((), (), s32[]{:S(2)}) async-start(), calls=%async_computation.4 | async-start | bytes 3620864 | tf_op jit(solution)/shard_map/all_gather | solution.py:35
  7.9 90.4 %all-gather.3.cloned.1.call-start = ((), (), s32[]{:S(2)}) async-start(), calls=%async_computation.2 | async-start | bytes 1179648 | tf_op jit(solution)/shard_map/all_gather | solution.py:22
  8.7 10.0 %copy-start.3 = (s32[1,1,156]{2,1,0:T(1,128)S(1)}, s32[1,1,156]{2,1,0:T(1,128)}, u32[]{:S(2)}) copy-start(s32[1,1,156]{2,1,0:T(1,128)} %param.11) | copy-start | bytes 1876
  8.7 175.2 %all-reduce.5.cloned.1.call-start = ((), (), s32[]{:S(2)}) async-start(), calls=%async_computation.5 | async-start | bytes 524288 | tf_op jit(solution)/shard_map/psum | solution.py:47
  52.4 46.0 %copy-start.2 = (bf16[1024,64]{0,1:T(8,128)(2,1)S(1)}, bf16[1024,64]{0,1:T(8,128)(2,1)}, u32[]{:S(2)}) copy-start(bf16[1024,64]{0,1:T(8,128)(2,1)} %param.8) | copy-start | bytes 393220
  52.4 208.7 %reduce-scatter.9.cloned.1.call-start = ((), (), s32[]{:S(2)}) async-start(), calls=%async_computation.7 | async-start | bytes 2359296 | tf_op jit(solution)/shard_map/reduce_scatter | solution.py:46
  61.3 317.1 %all-reduce.3.cloned.1.call-start = ((), (), s32[]{:S(2)}) async-start(), calls=%async_computation.3 | async-start | bytes 524288 | tf_op jit(solution)/shard_map/psum | solution.py:30
  100.7 361.2 %reduce-scatter.7.cloned.1.call-start = ((), (), s32[]{:S(2)}) async-start(), calls=%async_computation.6 | async-start | bytes 7241728 | tf_op jit(solution)/shard_map/reduce_scatter | solution.py:29
  118.5 6.3 %copy-start.1 = (bf16[512,1024]{1,0:T(8,128)(2,1)S(1)}, bf16[512,1024]{1,0:T(8,128)(2,1)}, u32[]{:S(2)}) copy-start(bf16[512,1024]{1,0:T(8,128)(2,1)} %all-gather.3.cloned.1.call-done) | copy-start | bytes 3145732
Sparse Core Ops, SparseCore 0:
  9.7 38.8 all-gather.4
  51.0 47.3 all-gather.2
  100.8 82.9 all-reduce.4
  187.9 73.0 reduce-scatter.8
  263.4 114.9 all-reduce.2
  380.8 81.0 reduce-scatter.6
where the time goes:
time: 475 us; the launch traced here: 471 us
  waiting for transfers between devices  388 us (82%)
  matrix products  35.6 us (7%)
  local copies, waits for them, and re-layouts  26.1 us (5%)
  between operations  14.2 us (3%)
  other arithmetic  6.56 us (1%)
    psum x1, waiting for transfers between devices, body(): low = lax.psum(low_part, 'row')  115 us
    reduce_scatter x1, waiting for transfers between devices, body(): out_sum = lax.psum_scatter(out_part, 'row', scatter_dimension=0, tiled=True)  83.5 us
    reduce_scatter x1, waiting for transfers between devices, body(): in_sum = lax.psum_scatter(in_part, 'col', scatter_dimension=0, tiled=True)  77.2 us
    psum x1, waiting for transfers between devices, body(): grad_low = lax.psum(gradient_lowrank_partial, 'col')  50.2 us
    all_gather x1, waiting for transfers between devices, body(): x_all = lax.all_gather(tokens, 'col', axis=0, tiled=True)  37.1 us
    all_gather x1, waiting for transfers between devices, body(): dy_all = lax.all_gather(grad_out, 'row', axis=0, tiled=True)  23 us
    unnamed x14, local copies, waits for them, and re-layouts  19.6 us
    dot_general x1, matrix products, body(): out_part = jnp.dot(x_all, masked, preferred_element_type=jnp.float32)  9.77 us
  transfers between devices with their start and end apart: 6, of which 6 were waited for; matrix products, arithmetic and copies ran while one was open for 14% of the time, Pallas kernels for 0%

commit v1 on v0

v1 whole, which is shorter than its diff:
```python
import functools
import math

import jax
import jax.numpy as jnp
from jax import lax
from jax.experimental import pallas as pl
from jax.experimental.pallas import tpu as pltpu
from jax.sharding import PartitionSpec as P

MESH = pl.DeviceIdType.MESH
F32 = jnp.float32
BF16 = jnp.bfloat16
TILE = 256
P_CHUNKS = ((0, 4), (4, 3), (7, 3), (10, 3))
G_CHUNKS = ((0, 1), (1, 1), (2, 1), (3, 1))
N_SEM = 96


def dot(a, b):
    return jnp.dot(a, b, preferred_element_type=F32)


def dot_t(a, b):
    return lax.dot_general(a, b, (((1,), (1,)), ((), ())), preferred_element_type=F32)


def split_terms(twice):
    first = lax.broadcasted_iota(jnp.int32, twice.shape, 1) < twice.shape[1] // 2
    high = twice.astype(BF16).astype(F32)
    rest = twice - high
    middle = rest.astype(BF16).astype(F32)
    low = rest - middle
    return (jnp.where(first, high, middle).astype(BF16), jnp.where(first, low, 0.0).astype(BF16))


def kernel(x_in, w_in, down, up, dy_in, tiles, out, gx_out, gw_out,
           x_all, dy_all, w, mask, up_ext, down_ext, x_low, dy_low, x_t, gw,
           p, p_sib, p_h1, p_h2, p_z, q, q_h1, q_h2, q_z, send, recv, local):
    r = lax.axis_index("row")
    c = lax.axis_index("col")
    core = lax.rem(r, 2)
    y, zl = r // 4, lax.rem(r // 2, 2)
    x, zh = c // 2, lax.rem(c, 2)
    rz, rs = r + 2 - 4 * zl, r + 1 - 2 * core
    rl, rr, ro = lax.rem(r + 12, 16), lax.rem(r + 4, 16), lax.rem(r + 8, 16)
    rlz, rrz, roz = lax.rem(rz + 12, 16), lax.rem(rz + 4, 16), lax.rem(rz + 8, 16)
    cz = c + 1 - 2 * zh
    cl, cr, co = lax.rem(c + 6, 8), lax.rem(c + 2, 8), lax.rem(c + 4, 8)
    clz, crz, coz = lax.rem(cz + 6, 8), lax.rem(cz + 2, 8), lax.rem(cz + 4, 8)
    sib, y_left, y_right, z_low = (rs, c), (rl, c), (rr, c), (rz, c)
    x_left, x_right, z_high = (r, cl), (r, cr), (r, cz)

    counter = [0]
    sends = []

    def ident():
        counter[0] += 1
        return counter[0] - 1

    def put(i, src, dst, device):
        copy = pltpu.make_async_remote_copy(
            src_ref=src, dst_ref=dst, send_sem=send.at[i], recv_sem=recv.at[i],
            device_id=device, device_id_type=MESH)
        copy.start()
        sends.append(copy)

    def got(i, dst):
        pltpu.make_async_remote_copy(
            src_ref=dst, dst_ref=dst, send_sem=send.at[i], recv_sem=recv.at[i],
            device_id=sib, device_id_type=MESH).wait_recv()

    w_copy = pltpu.make_async_copy(w_in, w, local.at[0])
    w_copy.start()
    x_copy = pltpu.make_async_copy(x_in, x_all.at[c], local.at[1])
    x_copy.start()
    dy_copy = pltpu.make_async_copy(dy_in, dy_all.at[r], local.at[2])
    dy_copy.start()

    barrier = pltpu.get_barrier_semaphore()
    for device in (sib, y_left, y_right, z_low, x_left, x_right, z_high):
        pl.semaphore_signal(barrier, inc=1, device_id=device, device_id_type=MESH)
    pl.semaphore_wait(barrier, 7)

    x0, x1r, x1l, x2r, x2l, x3r, x3l, x4r, x4l = (ident() for _ in range(9))
    d0, d1r, d1l, d2r, d2l, d3r, d3l, d4r, d4l = (ident() for _ in range(9))
    s = [ident() for _ in range(10)]
    put(x0, x_in, x_all.at[c], z_high)
    put(x1r, x_in, x_all.at[c], x_right)
    put(x1l, x_in, x_all.at[c], x_left)
    put(d0, dy_in, dy_all.at[r], z_low)
    put(d1r, dy_in, dy_all.at[r], y_right)
    put(d1l, dy_in, dy_all.at[r], y_left)
    put(s[0], dy_in, dy_all.at[r], sib)

    listed = tiles[...]
    number = lax.broadcasted_iota(jnp.int32, (8, listed.shape[1]), 0) * 26
    for tile in range(26):
        hit = jnp.where(jnp.broadcast_to(listed, number.shape) == number + tile, 1.0, 0.0)
        flag = jnp.sum(hit, axis=1, keepdims=True)
        mask[:, tile * 128:(tile + 1) * 128] = jnp.broadcast_to(flag, (8, 128))

    d = down[...].astype(F32)
    twice = jnp.concatenate([d, d], axis=1)
    first = lax.broadcasted_iota(jnp.int32, twice.shape, 1) < 64
    down_ext[:, :128] = twice.astype(BF16)
    down_ext[:, 128:] = jnp.where(first, twice, 0.0).astype(BF16)
    for part in range(3):
        up_ext[64 * part:64 * (part + 1), :] = up[...]
    up_ext[192:, :] = jnp.zeros_like(up)

    got(x0, x_all.at[cz])
    put(x2r, x_all.at[cz], x_all.at[cz], x_right)
    put(x2l, x_all.at[cz], x_all.at[cz], x_left)
    got(x1r, x_all.at[cl])
    put(x3r, x_all.at[cl, 0], x_all.at[cl, 0], x_right)
    got(x1l, x_all.at[cr])
    put(x3l, x_all.at[cr, 1], x_all.at[cr, 1], x_left)

    w_copy.wait()

    def masking(step, carry):
        at = pl.ds(pl.multiple_of(step * TILE, TILE), TILE)
        for block in range(8):
            rows = slice(block * 128, (block + 1) * 128)
            keep = mask[block:block + 1, at].astype(BF16)
            w[rows, at] = w[rows, at] * jnp.broadcast_to(keep, (128, TILE))
        return carry

    lax.fori_loop(0, 13, masking, 0)

    got(d0, dy_all.at[rz])
    put(d2r, dy_all.at[rz], dy_all.at[rz], y_right)
    put(d2l, dy_all.at[rz], dy_all.at[rz], y_left)
    put(s[1], dy_all.at[rz], dy_all.at[rz], sib)
    got(x2r, x_all.at[clz])
    put(x4r, x_all.at[clz, 0], x_all.at[clz, 0], x_right)
    got(x2l, x_all.at[crz])
    put(x4l, x_all.at[crz, 1], x_all.at[crz, 1], x_left)
    got(d1r, dy_all.at[rl])
    put(d3r, dy_all.at[rl, 0], dy_all.at[rl, 0], y_right)
    put(s[2], dy_all.at[rl], dy_all.at[rl], sib)
    got(d1l, dy_all.at[rr])
    put(d3l, dy_all.at[rr, 1], dy_all.at[rr, 1], y_left)
    put(s[3], dy_all.at[rr], dy_all.at[rr], sib)
    got(x3r, x_all.at[co, 0])
    got(x3l, x_all.at[co, 1])
    got(x4r, x_all.at[coz, 0])
    got(x4l, x_all.at[coz, 1])
    x_copy.wait()

    def x_rows():
        return x_all[...].reshape(512, 1024)

    parts = split_terms(dot(x_rows(), down_ext[:, :128]))
    x_low[:, :128] = parts[0]
    x_low[:, 128:] = parts[1]

    p_ids = [[ident() for _ in range(5)] for _ in P_CHUNKS]
    q_ids = [[ident() for _ in range(5)] for _ in G_CHUNKS]

    def span(chunk):
        return slice(chunk[0] * TILE, (chunk[0] + chunk[1]) * TILE)

    def p_compute(n):
        def step(i, carry):
            at = pl.ds(pl.multiple_of(i * TILE, TILE), TILE)
            value = dot(x_rows(), w[:, at]) + dot(x_low[...], up_ext[:, at])
            p[:, :, :, :, at] = value.reshape(4, 2, 2, 32, TILE)
            return carry

        first, count = P_CHUNKS[n]
        lax.fori_loop(first, first + count, step, 0)
        at = span(P_CHUNKS[n])
        put(p_ids[n][0], p.at[:, :, 1 - core, :, at], p_sib.at[:, :, :, at], sib)

    def p_pair(n):
        at = span(P_CHUNKS[n])
        got(p_ids[n][0], p_sib.at[:, :, :, at])
        p[:, :, core, :, at] = p[:, :, core, :, at] + p_sib[:, :, :, at]
        first_hop(n, p_ids[n], lambda k: p.at[k, :, core, :, at], p_h1.at[:, :, at], p_h2.at[:, :, :, at], y, y_left, y_right)

    def first_hop(n, ids, view, h1, h2, k, left, right):
        far, lower, upper = lax.rem(k + 2, 4), lax.rem(k + 3, 4), lax.rem(k + 1, 4)
        if n % 2 == 0:
            put(ids[1], view(far), h1, left)
            put(ids[3], view(upper), h2.at[1], right)
        else:
            put(ids[1], view(far), h1, right)
            put(ids[2], view(lower), h2.at[0], left)

    def second_hop(n, ids, view, h1, h2, k, left, right):
        lower, upper = lax.rem(k + 3, 4), lax.rem(k + 1, 4)
        got(ids[1], h1)
        target = view(lower) if n % 2 == 0 else view(upper)
        target[...] = target[...] + h1[...]
        if n % 2 == 0:
            put(ids[2], target, h2.at[0], left)
        else:
            put(ids[3], target, h2.at[1], right)

    def third_hop(n, ids, view, h2, z, k, other, device):
        got(ids[2], h2.at[0])
        got(ids[3], h2.at[1])
        total = view(k)
        total[...] = total[...] + h2[0] + h2[1]
        put(ids[4], total.at[other], z, device)

    def p_second(n):
        at = span(P_CHUNKS[n])
        second_hop(n, p_ids[n], lambda k: p.at[k, :, core, :, at], p_h1.at[:, :, at], p_h2.at[:, :, :, at], y, y_left, y_right)

    def p_third(n):
        at = span(P_CHUNKS[n])
        third_hop(n, p_ids[n], lambda k: p.at[k, :, core, :, at], p_h2.at[:, :, :, at], p_z.at[:, at], y, 1 - zl, z_low)

    def p_last(n):
        at = span(P_CHUNKS[n])
        got(p_ids[n][4], p_z.at[:, at])
        out[:, at] = (p[y, zl, core, :, at] + p_z[:, at]).astype(BF16)

    def q_compute(n):
        at = span(G_CHUNKS[n])
        value = dot_t(dy_all[...].reshape(512, 3328), w[at, :]) + dot_t(dy_low[...], down_ext[at, :])
        q[:, :, :, at] = value.reshape(4, 2, 64, value.shape[1])
        first_hop(n, q_ids[n], lambda k: q.at[k, :, :, at], q_h1.at[:, :, at], q_h2.at[:, :, :, at], x, x_left, x_right)

    def q_second(n):
        at = span(G_CHUNKS[n])
        second_hop(n, q_ids[n], lambda k: q.at[k, :, :, at], q_h1.at[:, :, at], q_h2.at[:, :, :, at], x, x_left, x_right)

    def q_third(n):
        at = span(G_CHUNKS[n])
        third_hop(n, q_ids[n], lambda k: q.at[k, :, :, at], q_h2.at[:, :, :, at], q_z.at[:, at], x, 1 - zh, z_high)

    def q_last(n):
        at = span(G_CHUNKS[n])
        got(q_ids[n][4], q_z.at[:, at])
        gx_out[:, at] = (q[x, zh, :, at] + q_z[:, at]).astype(BF16)

    gw_copies = []

    def gw_compute(first, last):
        def step(i, carry):
            at = pl.ds(pl.multiple_of(i * TILE, TILE), TILE)
            for half in range(2):
                rows = slice(half * 512, (half + 1) * 512)
                value = dot(x_t[rows, :], dy_all[:, :, :, at].reshape(512, TILE))
                for block in range(4):
                    keep = mask[half * 4 + block:half * 4 + block + 1, at] * (1.0 / math.sqrt(512))
                    gw[half * 512 + block * 128:half * 512 + (block + 1) * 128, at] = (
                        value[block * 128:(block + 1) * 128] * keep).astype(BF16)
            return carry

        lax.fori_loop(first, last, step, 0)
        at = slice(first * TILE, last * TILE)
        copy = pltpu.make_async_copy(gw.at[:, at], gw_out.at[:, at], local.at[3 + len(gw_copies)])
        copy.start()
        gw_copies.append(copy)

    p_compute(0)
    p_compute(1)
    p_pair(0)
    got(d2r, dy_all.at[rlz])
    put(d4r, dy_all.at[rlz, 0], dy_all.at[rlz, 0], y_right)
    put(s[4], dy_all.at[rlz], dy_all.at[rlz], sib)
    got(d2l, dy_all.at[rrz])
    put(d4l, dy_all.at[rrz, 1], dy_all.at[rrz, 1], y_left)
    put(s[5], dy_all.at[rrz], dy_all.at[rrz], sib)
    p_compute(2)
    p_pair(1)
    got(d3r, dy_all.at[ro, 0])
    put(s[6], dy_all.at[ro, 0], dy_all.at[ro, 0], sib)
    got(d3l, dy_all.at[ro, 1])
    put(s[7], dy_all.at[ro, 1], dy_all.at[ro, 1], sib)
    p_compute(3)
    p_pair(2)
    for quarter in range(4):
        cols = slice(quarter * 256, (quarter + 1) * 256)
        x_t[cols, :] = x_all[:, :, :, cols].reshape(512, 256).T
    p_pair(3)
    got(d4r, dy_all.at[roz, 0])
    put(s[8], dy_all.at[roz, 0], dy_all.at[roz, 0], sib)
    got(d4l, dy_all.at[roz, 1])
    put(s[9], dy_all.at[roz, 1], dy_all.at[roz, 1], sib)

    dy_copy.wait()
    for i, index in enumerate((r, rz, rl, rr, rlz, rrz)):
        got(s[i], dy_all.at[index + 1 - 2 * core])
    for i, index in enumerate((ro, roz)):
        for half in range(2):
            got(s[6 + 2 * i + half], dy_all.at[index + 1 - 2 * core, half])

    parts = split_terms(dot_t(dy_all[...].reshape(512, 3328), up_ext[:128, :]))
    dy_low[:, :128] = parts[0]
    dy_low[:, 128:] = parts[1]

    q_compute(0)
    p_second(0)
    q_compute(1)
    p_second(1)
    q_second(0)
    q_compute(2)
    p_second(2)
    q_second(1)
    q_compute(3)
    p_second(3)
    q_second(2)
    gw_compute(0, 3)
    p_third(0)
    q_second(3)
    gw_compute(3, 6)
    q_third(0)
    p_third(1)
    gw_compute(6, 9)
    q_third(1)
    p_third(2)
    gw_compute(9, 11)
    q_third(2)
    gw_compute(11, 13)
    q_third(3)
    for n in range(4):
        q_last(n)
    p_third(3)
    for n in range(4):
        p_last(n)
    for copy in gw_copies:
        copy.wait()
    for copy in sends:
        copy.wait_send()


def body(tokens, weight, down, up, grad_out, tile_list):
    anywhere = pl.BlockSpec(memory_space=pl.ANY)
    vmem = pl.BlockSpec(memory_space=pltpu.VMEM)
    scratch = [
        pltpu.VMEM((8, 2, 32, 1024), BF16),
        pltpu.VMEM((16, 2, 16, 3328), BF16),
        pltpu.VMEM((1024, 3328), BF16),
        pltpu.VMEM((8, 3328), F32),
        pltpu.VMEM((256, 3328), BF16),
        pltpu.VMEM((1024, 256), BF16),
        pltpu.VMEM((512, 256), BF16),
        pltpu.VMEM((512, 256), BF16),
        pltpu.VMEM((1024, 512), BF16),
        pltpu.VMEM((1024, 3328), BF16),
        pltpu.VMEM((4, 2, 2, 32, 3328), F32),
        pltpu.VMEM((4, 2, 32, 3328), F32),
        pltpu.VMEM((2, 32, 3328), F32),
        pltpu.VMEM((2, 2, 32, 3328), F32),
        pltpu.VMEM((32, 3328), F32),
        pltpu.VMEM((4, 2, 64, 1024), F32),
        pltpu.VMEM((2, 64, 1024), F32),
        pltpu.VMEM((2, 2, 64, 1024), F32),
        pltpu.VMEM((64, 1024), F32),
        pltpu.SemaphoreType.DMA((N_SEM,)),
        pltpu.SemaphoreType.DMA((N_SEM,)),
        pltpu.SemaphoreType.DMA((8,)),
    ]
    return pl.pallas_call(
        kernel,
        out_shape=(
            jax.ShapeDtypeStruct((32, 3328), BF16),
            jax.ShapeDtypeStruct((64, 1024), BF16),
            jax.ShapeDtypeStruct((1024, 3328), BF16),
        ),
        in_specs=[anywhere, anywhere, vmem, vmem, anywhere, vmem],
        out_specs=(vmem, vmem, anywhere),
        scratch_shapes=scratch,
        compiler_params=pltpu.CompilerParams(
            collective_id=0, has_side_effects=True, vmem_limit_bytes=60 * 2**20),
        cost_estimate=pl.CostEstimate(flops=3 * 2 * 512 * 1024 * 3328, bytes_accessed=14 * 2**20, transcendentals=0),
    )(tokens.reshape(2, 32, 1024), weight, down, up, grad_out.reshape(2, 16, 3328), tile_list.reshape(1, -1))


def solution(mesh):
    return jax.shard_map(
        body,
        mesh=mesh,
        in_specs=(
            P("col", "row"),
            P("row", "col"),
            P("row", None),
            P(None, "col"),
            P("row", "col"),
            P("row", "col", None),
        ),
        out_specs=(P("row", "col"), P("col", "row"), P("row", "col")),
        check_vma=False,
    )
```

time: 475 us -> 89.9 us (0.19)
  waiting for transfers between devices: 388 us -> 0 us
  Pallas kernels: 0 us -> 77.9 us
  matrix products: 35.6 us -> 0 us
  local copies, waits for them, and re-layouts: 26.1 us -> 11.2 us
  between operations: 14.2 us -> 0.64 us
  other arithmetic: 6.56 us -> 0 us
    psum x2 -> x0, waiting for transfers between devices: 166 us -> none  [the longest x1 115 us: body(): low = lax.psum(low_part, 'row')]
    reduce_scatter x2 -> x0, waiting for transfers between devices: 161 us -> none  [the longest x1 83.5 us: body(): out_sum = lax.psum_scatter(out_part, 'row', scatter_dimension=0, tiled=True)]
    pallas_call x0 -> x1, Pallas kernels: none -> 77.9 us  [body(): pl.pallas_call(kernel, out_shape=(jax.ShapeDtypeStruct((32, 3328), BF16),...]
    all_gather x2 -> x0, waiting for transfers between devices: 60.1 us -> none  [the longest x1 37.1 us: body(): x_all = lax.all_gather(tokens, 'col', axis=0, tiled=True)]
    dot_general x7 -> x0, matrix products: 35.6 us -> none  [the longest x1 9.77 us: body(): out_part = jnp.dot(x_all, masked, preferred_element_type=jnp.float32)]
    unnamed x14 -> x4, local copies, waits for them, and re-layouts: 19.6 us -> 11.2 us
    mul x1 -> x0, other arithmetic: 6.46 us -> none  [body(): masked = weight * mask]
    reshape x3 -> x0, local copies, waits for them, and re-layouts: 5.63 us -> none  [the longest x1 5.42 us: body(): jnp.repeat(jnp.repeat(grid, side, axis=0), side, axis=1)]
  transfers between devices with their start and end apart: 6 -> 0, of which waited for: 6 -> 0; matrix products, arithmetic and copies ran while one was open for 14% -> 0% of each run, Pallas kernels for 0% -> 0%
where the time goes in v1:
time: 89.9 us; the launch traced here: 89.7 us
  Pallas kernels  77.9 us (87%)
  local copies, waits for them, and re-layouts  11.2 us (12%)
    pallas_call x1, Pallas kernels, body(): pl.pallas_call(kernel, out_shape=(jax.ShapeDtypeStruct((32, 3328), BF16),...  77.9 us
    unnamed x4, local copies, waits for them, and re-layouts  11.2 us

profile of v1, /device:TPU:0, one launch (start us, length us, event | category | flops | bytes accessed | tf_op | source)
XLA Modules:
  0.0 89.7 jit_solution(10968588822395793318)
XLA Ops:
  0.6 1.7 %copy.9.down = bf16[1024,64]{1,0:T(8,128)(2,1)} copy(bf16[1024,64]{0,1:T(8,128)(2,1)} %param.8) | data formatting | bytes 262144 | tf_op args[2]
  2.4 77.9 %shard_map.85 = (bf16[32,3328]{1,0:T(8,128)(2,1)}, bf16[64,1024]{1,0:T(8,128)(2,1)}, bf16[1024,3328]{1,0:T(8,128)(2,1)}) custom-call(bf16[2,32,1024]{2,1,0:T(8,128)(2,1)} %bitcast.4, bf16[1024,3328]{1,0:T(8,128)(2,1)} %w_in.1, bf16[1024,64]{1,0:T(8,128)(2,1)} %copy.9.down, bf16[64,3328]{1,0:T(8,128)(2,1)} %up.1, bf16[2,16,3328]{2,1,0:T(8,128)(2,1)} %bitcast.3, ...), custom_call_target="tpu_custom_call" | custom-call | flops 10468982784 | bytes 14680064 | tf_op jit(solution)/shard_map/pallas_call | solution.py:360
  80.2 1.6 %copy.13 = bf16[32,3328]{1,0:T(8,128)(2,1)} copy(bf16[32,3328]{1,0:T(8,128)(2,1)} %get-tuple-element.6) | data formatting | bytes 425984
  81.9 1.6 %copy.14 = bf16[64,1024]{1,0:T(8,128)(2,1)} copy(bf16[64,1024]{1,0:T(8,128)(2,1)} %get-tuple-element.7) | data formatting | bytes 262144
  83.4 6.2 %copy.15 = bf16[1024,3328]{1,0:T(8,128)(2,1)} copy(bf16[1024,3328]{1,0:T(8,128)(2,1)} %get-tuple-element.8) | data formatting | bytes 13631488

commit v2 on v1

--- a/solution.py
+++ b/solution.py
@@ -11,6 +11,7 @@
 MESH = pl.DeviceIdType.MESH
 F32 = jnp.float32
 BF16 = jnp.bfloat16
+I16 = jnp.int16
 TILE = 256
 P_CHUNKS = ((0, 4), (4, 3), (7, 3), (10, 3))
 G_CHUNKS = ((0, 1), (1, 1), (2, 1), (3, 1))
@@ -34,9 +35,29 @@
     return (jnp.where(first, high, middle).astype(BF16), jnp.where(first, low, 0.0).astype(BF16))
 
 
-def kernel(x_in, w_in, down, up, dy_in, tiles, out, gx_out, gw_out,
-           x_all, dy_all, w, mask, up_ext, down_ext, x_low, dy_low, x_t, gw,
-           p, p_sib, p_h1, p_h2, p_z, q, q_h1, q_h2, q_z, send, recv, local):
+def diagonal(rows):
+    shape = (rows, 128)
+    return lax.broadcasted_iota(jnp.int32, shape, 0) == lax.broadcasted_iota(jnp.int32, shape, 1)
+
+
+def encode(value, code, scale):
+    value = value.reshape(code.shape)
+    top = jnp.maximum(jnp.max(jnp.abs(value), axis=1, keepdims=True), 1e-30)
+    code[...] = jnp.round(value * (32760.0 / top)).astype(jnp.int32).astype(jnp.int16)
+    row = jnp.sum(jnp.where(diagonal(code.shape[0]), top * (1.0 / 32760.0), 0.0), axis=0, keepdims=True)
+    scale[...] = jnp.broadcast_to(row, (8, 128))
+
+
+def decode(code, scale, shape):
+    rows = code.shape[0]
+    row = jnp.broadcast_to(scale[0:1, :], (rows, 128))
+    column = jnp.sum(jnp.where(diagonal(rows), row, 0.0), axis=1, keepdims=True)
+    return (code[...].astype(jnp.int32).astype(F32) * column).reshape(shape)
+
+
+def kernel(x_in, w_in, down_in, up_in, dy_in, tiles_in, out, gx_out, gw,
+           x_all, dy_all, w, tiles, mask, up_ext, down_ext, x_low, dy_low, x_t,
+           p, p_sib, p_out, p_in, pz_out, pz_in, q, q_out, q_in, qz_out, qz_in, scale_out, scale_in, send, recv, local):
     r = lax.axis_index("row")
     c = lax.axis_index("col")
     core = lax.rem(r, 2)
@@ -77,6 +98,14 @@
     dy_copy = pltpu.make_async_copy(dy_in, dy_all.at[r], local.at[2])
     dy_copy.start()
 
+    small = [pltpu.make_async_copy(tiles_in, tiles, local.at[3])]
+    for part in range(3):
+        rows = slice(64 * part, 64 * (part + 1))
+        small.append(pltpu.make_async_copy(down_in, down_ext.at[rows], local.at[4 + part]))
+        small.append(pltpu.make_async_copy(up_in, up_ext.at[rows], local.at[7 + part]))
+    for copy in small:
+        copy.start()
+
     barrier = pltpu.get_barrier_semaphore()
     for device in (sib, y_left, y_right, z_low, x_left, x_right, z_high):
         pl.semaphore_signal(barrier, inc=1, device_id=device, device_id_type=MESH)
@@ -88,11 +117,11 @@
     put(x0, x_in, x_all.at[c], z_high)
     put(x1r, x_in, x_all.at[c], x_right)
     put(x1l, x_in, x_all.at[c], x_left)
-    put(d0, dy_in, dy_all.at[r], z_low)
     put(d1r, dy_in, dy_all.at[r], y_right)
     put(d1l, dy_in, dy_all.at[r], y_left)
     put(s[0], dy_in, dy_all.at[r], sib)
 
+    small[0].wait()
     listed = tiles[...]
     number = lax.broadcasted_iota(jnp.int32, (8, listed.shape[1]), 0) * 26
     for tile in range(26):
@@ -100,22 +129,30 @@
         flag = jnp.sum(hit, axis=1, keepdims=True)
         mask[:, tile * 128:(tile + 1) * 128] = jnp.broadcast_to(flag, (8, 128))
 
-    d = down[...].astype(F32)
-    twice = jnp.concatenate([d, d], axis=1)
-    first = lax.broadcasted_iota(jnp.int32, twice.shape, 1) < 64
-    down_ext[:, :128] = twice.astype(BF16)
-    down_ext[:, 128:] = jnp.where(first, twice, 0.0).astype(BF16)
-    for part in range(3):
-        up_ext[64 * part:64 * (part + 1), :] = up[...]
-    up_ext[192:, :] = jnp.zeros_like(up)
+    down_ext[192:, :] = jnp.zeros((64, 1024), BF16)
+    up_ext[192:, :] = jnp.zeros((64, 3328), BF16)
+    for copy in small[1:]:
+        copy.wait()
 
     got(x0, x_all.at[cz])
     put(x2r, x_all.at[cz], x_all.at[cz], x_right)
     put(x2l, x_all.at[cz], x_all.at[cz], x_left)
+    put(d0, dy_in, dy_all.at[r], z_low)
     got(x1r, x_all.at[cl])
     put(x3r, x_all.at[cl, 0], x_all.at[cl, 0], x_right)
     got(x1l, x_all.at[cr])
     put(x3l, x_all.at[cr, 1], x_all.at[cr, 1], x_left)
+
+    got(d1r, dy_all.at[rl])
+    put(d3r, dy_all.at[rl, 0], dy_all.at[rl, 0], y_right)
+    put(s[2], dy_all.at[rl], dy_all.at[rl], sib)
+    got(d1l, dy_all.at[rr])
+    put(d3l, dy_all.at[rr, 1], dy_all.at[rr, 1], y_left)
+    put(s[3], dy_all.at[rr], dy_all.at[rr], sib)
+    got(x2r, x_all.at[clz])
+    put(x4r, x_all.at[clz, 0], x_all.at[clz, 0], x_right)
+    got(x2l, x_all.at[crz])
+    put(x4l, x_all.at[crz, 1], x_all.at[crz, 1], x_left)
 
     w_copy.wait()
 
@@ -133,16 +170,6 @@
     put(d2r, dy_all.at[rz], dy_all.at[rz], y_right)
     put(d2l, dy_all.at[rz], dy_all.at[rz], y_left)
     put(s[1], dy_all.at[rz], dy_all.at[rz], sib)
-    got(x2r, x_all.at[clz])
-    put(x4r, x_all.at[clz, 0], x_all.at[clz, 0], x_right)
-    got(x2l, x_all.at[crz])
-    put(x4l, x_all.at[crz, 1], x_all.at[crz, 1], x_left)
-    got(d1r, dy_all.at[rl])
-    put(d3r, dy_all.at[rl, 0], dy_all.at[rl, 0], y_right)
-    put(s[2], dy_all.at[rl], dy_all.at[rl], sib)
-    got(d1l, dy_all.at[rr])
-    put(d3l, dy_all.at[rr, 1], dy_all.at[rr, 1], y_left)
-    put(s[3], dy_all.at[rr], dy_all.at[rr], sib)
     got(x3r, x_all.at[co, 0])
     got(x3l, x_all.at[co, 1])
     got(x4r, x_all.at[coz, 0])
@@ -152,12 +179,11 @@
     def x_rows():
         return x_all[...].reshape(512, 1024)
 
-    parts = split_terms(dot(x_rows(), down_ext[:, :128]))
+    parts = split_terms(dot_t(x_rows(), down_ext[:128, :]))
     x_low[:, :128] = parts[0]
     x_low[:, 128:] = parts[1]
 
-    p_ids = [[ident() for _ in range(5)] for _ in P_CHUNKS]
-    q_ids = [[ident() for _ in range(5)] for _ in G_CHUNKS]
+    p_sib_ids = [ident() for _ in P_CHUNKS]
 
     def span(chunk):
         return slice(chunk[0] * TILE, (chunk[0] + chunk[1]) * TILE)
@@ -172,73 +198,91 @@
         first, count = P_CHUNKS[n]
         lax.fori_loop(first, first + count, step, 0)
         at = span(P_CHUNKS[n])
-        put(p_ids[n][0], p.at[:, :, 1 - core, :, at], p_sib.at[:, :, :, at], sib)
+        put(p_sib_ids[n], p.at[:, :, 1 - core, :, at], p_sib.at[:, :, :, at], sib)
+
+    def ring_sum(chunks, view, shape, out_codes, in_codes, z_out, z_in, k, other, left, right, z_device, finish):
+        far, lower, upper = lax.rem(k + 2, 4), lax.rem(k + 3, 4), lax.rem(k + 1, 4)
+        ids = [[(ident(), ident(), scale_id()) for _ in range(4)] for _ in chunks]
+
+        def post(n, hop, value, code_out, code_in, device):
+            data, scales, slot = ids[n][hop]
+            encode(value, code_out, scale_out.at[slot])
+            put(data, code_out, code_in, device)
+            put(scales, scale_out.at[slot], scale_in.at[slot], device)
+
+        def take(n, hop, code_in, to):
+            data, scales, slot = ids[n][hop]
+            got(data, code_in)
+            got(scales, scale_in.at[slot])
+            return decode(code_in, scale_in.at[slot], to)
+
+        def block(n):
+            at = span(chunks[n])
+            return at, shape + (at.stop - at.start,)
+
+        def first(n):
+            at, _ = block(n)
+            post(n, 0, view(far, at)[...], out_codes.at[0, :, at], in_codes.at[0, :, at], (left, right)[n % 2])
+            if n % 2 == 0:
+                post(n, 2, view(upper, at)[...], out_codes.at[2, :, at], in_codes.at[2, :, at], right)
+            else:
+                post(n, 1, view(lower, at)[...], out_codes.at[1, :, at], in_codes.at[1, :, at], left)
+
+        def second(n):
+            at, to = block(n)
+            came = take(n, 0, in_codes.at[0, :, at], to)
+            if n % 2 == 0:
+                post(n, 1, view(lower, at)[...] + came, out_codes.at[1, :, at], in_codes.at[1, :, at], left)
+            else:
+                post(n, 2, view(upper, at)[...] + came, out_codes.at[2, :, at], in_codes.at[2, :, at], right)
+
+        def third(n):
+            at, to = block(n)
+            total = view(k, at)
+            total[...] = (total[...] + take(n, 1, in_codes.at[1, :, at], to)
+                          + take(n, 2, in_codes.at[2, :, at], to))
+            post(n, 3, total[other], z_out.at[:, at], z_in.at[:, at], z_device)
+
+        def last(n):
+            at, to = block(n)
+            finish(at, view(k, at)[1 - other] + take(n, 3, z_in.at[:, at], to[1:]))
+
+        return first, second, third, last
+
+    scale_counter = [0]
+
+    def scale_id():
+        scale_counter[0] += 1
+        return scale_counter[0] - 1
+
+    def p_view(k, at):
+        return p.at[k, :, core, :, at]
+
+    def p_finish(at, value):
+        out[:, at] = value.astype(BF16)
+
+    def q_view(k, at):
+        return q.at[k, :, :, at]
+
+    def q_finish(at, value):
+        gx_out[:, at] = value.astype(BF16)
+
+    p_first, p_second, p_third, p_last = ring_sum(
+        P_CHUNKS, p_view, (2, 32), p_out, p_in, pz_out, pz_in, y, 1 - zl, y_left, y_right, z_low, p_finish)
+    q_first, q_second, q_third, q_last = ring_sum(
+        G_CHUNKS, q_view, (2, 64), q_out, q_in, qz_out, qz_in, x, 1 - zh, x_left, x_right, z_high, q_finish)
 
     def p_pair(n):
         at = span(P_CHUNKS[n])
-        got(p_ids[n][0], p_sib.at[:, :, :, at])
+        got(p_sib_ids[n], p_sib.at[:, :, :, at])
         p[:, :, core, :, at] = p[:, :, core, :, at] + p_sib[:, :, :, at]
-        first_hop(n, p_ids[n], lambda k: p.at[k, :, core, :, at], p_h1.at[:, :, at], p_h2.at[:, :, :, at], y, y_left, y_right)
-
-    def first_hop(n, ids, view, h1, h2, k, left, right):
-        far, lower, upper = lax.rem(k + 2, 4), lax.rem(k + 3, 4), lax.rem(k + 1, 4)
-        if n % 2 == 0:
-            put(ids[1], view(far), h1, left)
-            put(ids[3], view(upper), h2.at[1], right)
-        else:
-            put(ids[1], view(far), h1, right)
-            put(ids[2], view(lower), h2.at[0], left)
-
-    def second_hop(n, ids, view, h1, h2, k, left, right):
-        lower, upper = lax.rem(k + 3, 4), lax.rem(k + 1, 4)
-        got(ids[1], h1)
-        target = view(lower) if n % 2 == 0 else view(upper)
-        target[...] = target[...] + h1[...]
-        if n % 2 == 0:
-            put(ids[2], target, h2.at[0], left)
-        else:
-            put(ids[3], target, h2.at[1], right)
-
-    def third_hop(n, ids, view, h2, z, k, other, device):
-        got(ids[2], h2.at[0])
-        got(ids[3], h2.at[1])
-        total = view(k)
-        total[...] = total[...] + h2[0] + h2[1]
-        put(ids[4], total.at[other], z, device)
-
-    def p_second(n):
-        at = span(P_CHUNKS[n])
-        second_hop(n, p_ids[n], lambda k: p.at[k, :, core, :, at], p_h1.at[:, :, at], p_h2.at[:, :, :, at], y, y_left, y_right)
-
-    def p_third(n):
-        at = span(P_CHUNKS[n])
-        third_hop(n, p_ids[n], lambda k: p.at[k, :, core, :, at], p_h2.at[:, :, :, at], p_z.at[:, at], y, 1 - zl, z_low)
-
-    def p_last(n):
-        at = span(P_CHUNKS[n])
-        got(p_ids[n][4], p_z.at[:, at])
-        out[:, at] = (p[y, zl, core, :, at] + p_z[:, at]).astype(BF16)
+        p_first(n)
 
     def q_compute(n):
         at = span(G_CHUNKS[n])
-        value = dot_t(dy_all[...].reshape(512, 3328), w[at, :]) + dot_t(dy_low[...], down_ext[at, :])
+        value = dot_t(dy_all[...].reshape(512, 3328), w[at, :]) + dot(dy_low[...], down_ext[:, at])
         q[:, :, :, at] = value.reshape(4, 2, 64, value.shape[1])
-        first_hop(n, q_ids[n], lambda k: q.at[k, :, :, at], q_h1.at[:, :, at], q_h2.at[:, :, :, at], x, x_left, x_right)
-
-    def q_second(n):
-        at = span(G_CHUNKS[n])
-        second_hop(n, q_ids[n], lambda k: q.at[k, :, :, at], q_h1.at[:, :, at], q_h2.at[:, :, :, at], x, x_left, x_right)
-
-    def q_third(n):
-        at = span(G_CHUNKS[n])
-        third_hop(n, q_ids[n], lambda k: q.at[k, :, :, at], q_h2.at[:, :, :, at], q_z.at[:, at], x, 1 - zh, z_high)
-
-    def q_last(n):
-        at = span(G_CHUNKS[n])
-        got(q_ids[n][4], q_z.at[:, at])
-        gx_out[:, at] = (q[x, zh, :, at] + q_z[:, at]).astype(BF16)
-
-    gw_copies = []
+        q_first(n)
 
     def gw_compute(first, last):
         def step(i, carry):
@@ -253,10 +297,6 @@
             return carry
 
         lax.fori_loop(first, last, step, 0)
-        at = slice(first * TILE, last * TILE)
-        copy = pltpu.make_async_copy(gw.at[:, at], gw_out.at[:, at], local.at[3 + len(gw_copies)])
-        copy.start()
-        gw_copies.append(copy)
 
     p_compute(0)
     p_compute(1)
@@ -324,10 +364,18 @@
     p_third(3)
     for n in range(4):
         p_last(n)
-    for copy in gw_copies:
-        copy.wait()
     for copy in sends:
         copy.wait_send()
+
+
+def store(out, gx, gw, out_to, gx_to, gw_to, sems):
+    pairs = [(gw.at[pl.ds(128 * i, 128)], gw_to.at[pl.ds(128 * i, 128)]) for i in range(8)]
+    pairs += [(out, out_to), (gx, gx_to)]
+    copies = [pltpu.make_async_copy(src, dst, sems.at[i]) for i, (src, dst) in enumerate(pairs)]
+    for copy in copies:
+        copy.start()
+    for copy in copies:
+        copy.wait()
 
 
 def body(tokens, weight, down, up, grad_out, tile_list):
@@ -337,40 +385,50 @@
         pltpu.VMEM((8, 2, 32, 1024), BF16),
         pltpu.VMEM((16, 2, 16, 3328), BF16),
         pltpu.VMEM((1024, 3328), BF16),
+        pltpu.VMEM((1, 156), jnp.int32),
         pltpu.VMEM((8, 3328), F32),
         pltpu.VMEM((256, 3328), BF16),
-        pltpu.VMEM((1024, 256), BF16),
+        pltpu.VMEM((256, 1024), BF16),
         pltpu.VMEM((512, 256), BF16),
         pltpu.VMEM((512, 256), BF16),
         pltpu.VMEM((1024, 512), BF16),
-        pltpu.VMEM((1024, 3328), BF16),
         pltpu.VMEM((4, 2, 2, 32, 3328), F32),
         pltpu.VMEM((4, 2, 32, 3328), F32),
-        pltpu.VMEM((2, 32, 3328), F32),
-        pltpu.VMEM((2, 2, 32, 3328), F32),
-        pltpu.VMEM((32, 3328), F32),
+        pltpu.VMEM((3, 64, 3328), I16),
+        pltpu.VMEM((3, 64, 3328), I16),
+        pltpu.VMEM((32, 3328), I16),
+        pltpu.VMEM((32, 3328), I16),
         pltpu.VMEM((4, 2, 64, 1024), F32),
-        pltpu.VMEM((2, 64, 1024), F32),
-        pltpu.VMEM((2, 2, 64, 1024), F32),
-        pltpu.VMEM((64, 1024), F32),
+        pltpu.VMEM((3, 128, 1024), I16),
+        pltpu.VMEM((3, 128, 1024), I16),
+        pltpu.VMEM((64, 1024), I16),
+        pltpu.VMEM((64, 1024), I16),
+        pltpu.VMEM((32, 8, 128), F32),
+        pltpu.VMEM((32, 8, 128), F32),
         pltpu.SemaphoreType.DMA((N_SEM,)),
         pltpu.SemaphoreType.DMA((N_SEM,)),
-        pltpu.SemaphoreType.DMA((8,)),
+        pltpu.SemaphoreType.DMA((10,)),
     ]
-    return pl.pallas_call(
+    shapes = ((32, 3328), (64, 1024), (1024, 3328))
+    results = pl.pallas_call(
         kernel,
-        out_shape=(
-            jax.ShapeDtypeStruct((32, 3328), BF16),
-            jax.ShapeDtypeStruct((64, 1024), BF16),
-            jax.ShapeDtypeStruct((1024, 3328), BF16),
-        ),
-        in_specs=[anywhere, anywhere, vmem, vmem, anywhere, vmem],
-        out_specs=(vmem, vmem, anywhere),
+        out_shape=tuple(pltpu.VMEM(shape, BF16) for shape in shapes),
+        in_specs=[pl.BlockSpec(memory_space=pltpu.HBM)] * 6,
+        out_specs=(vmem, vmem, vmem),
         scratch_shapes=scratch,
         compiler_params=pltpu.CompilerParams(
-            collective_id=0, has_side_effects=True, vmem_limit_bytes=60 * 2**20),
+            collective_id=0, has_side_effects=True, vmem_limit_bytes=57 * 2**20),
         cost_estimate=pl.CostEstimate(flops=3 * 2 * 512 * 1024 * 3328, bytes_accessed=14 * 2**20, transcendentals=0),
-    )(tokens.reshape(2, 32, 1024), weight, down, up, grad_out.reshape(2, 16, 3328), tile_list.reshape(1, -1))
+    )(tokens.reshape(2, 32, 1024), weight, down.T, up, grad_out.reshape(2, 16, 3328), tile_list.reshape(1, -1))
+    return pl.pallas_call(
+        store,
+        out_shape=tuple(jax.ShapeDtypeStruct(shape, BF16) for shape in shapes),
+        in_specs=[vmem] * 3,
+        out_specs=(anywhere,) * 3,
+        scratch_shapes=[pltpu.SemaphoreType.DMA((10,))],
+        compiler_params=pltpu.CompilerParams(vmem_limit_bytes=2**20),
+        cost_estimate=pl.CostEstimate(flops=0, bytes_accessed=8 * 2**20, transcendentals=0),
+    )(*results)
 
 
 def solution(mesh):

time: 89.9 us -> 70.2 us (0.78)
  local copies, waits for them, and re-layouts: 11.2 us -> 0 us
  Pallas kernels: 77.9 us -> 69.5 us
    unnamed x4 -> x0, local copies, waits for them, and re-layouts: 11.2 us -> none
    pallas_call x1 -> x2, Pallas kernels: 77.9 us -> 69.5 us  [the longest x1 66.5 us: body(): pl.pallas_call(kernel, out_shape=tuple((pltpu.VMEM(shape, BF16) for shape...]
where the time goes in v2:
time: 70.2 us; the launch traced here: 70.1 us
  Pallas kernels  69.5 us (99%)
    pallas_call x1, Pallas kernels, body(): pl.pallas_call(kernel, out_shape=tuple((pltpu.VMEM(shape, BF16) for shape...  66.5 us
    pallas_call x1, Pallas kernels, body(): pl.pallas_call(store, out_shape=tuple((jax.ShapeDtypeStruct(shape, BF16)...  2.98 us

profile of v2, /device:TPU:0, one launch (start us, length us, event | category | flops | bytes accessed | tf_op | source)
XLA Modules:
  0.0 70.1 jit_solution(5012958821018767362)
XLA Ops:
  0.6 66.5 %shard_map.85 = (bf16[32,3328]{1,0:T(8,128)(2,1)S(1)}, bf16[64,1024]{1,0:T(8,128)(2,1)S(1)}, bf16[1024,3328]{1,0:T(8,128)(2,1)S(1)}) custom-call(bf16[2,32,1024]{2,1,0:T(8,128)(2,1)} %bitcast.5, bf16[1024,3328]{1,0:T(8,128)(2,1)} %w_in.1, bf16[64,1024]{1,0:T(8,128)(2,1)} %bitcast.6, bf16[64,3328]{1,0:T(8,128)(2,1)} %up_in.1, bf16[2,16,3328]{2,1,0:T(8,128)(2,1)} %bitcast.4, ...), custom_call_target="tpu_custom_call" | custom-call | flops 10468982784 | bytes 14680064 | tf_op jit(solution)/shard_map/pallas_call | solution.py:413
  67.1 3.0 %shard_map.86 = (bf16[32,3328]{1,0:T(8,128)(2,1)}, bf16[64,1024]{1,0:T(8,128)(2,1)}, bf16[1024,3328]{1,0:T(8,128)(2,1)}) custom-call(bf16[32,3328]{1,0:T(8,128)(2,1)S(1)} %get-tuple-element.6.out, bf16[64,1024]{1,0:T(8,128)(2,1)S(1)} %get-tuple-element.7.gx, bf16[1024,3328]{1,0:T(8,128)(2,1)S(1)} %get-tuple-element.8.gw), custom_call_target="tpu_custom_call" | custom-call | bytes 8388608 | tf_op jit(solution)/shard_map/pallas_call | solution.py:423

commit v3 on v2

v3 whole, which is shorter than its diff:
```python
import functools
import math

import jax
import jax.numpy as jnp
from jax import lax
from jax.experimental import pallas as pl
from jax.experimental.pallas import tpu as pltpu
from jax.sharding import PartitionSpec as P

MESH = pl.DeviceIdType.MESH
F32 = jnp.float32
BF16 = jnp.bfloat16
I16 = jnp.int16
TILE = 256
P_CHUNKS = ((0, 7), (7, 6))
G_CHUNKS = ((0, 2), (2, 2))
P_DIRECT, Q_DIRECT = False, True
N_SEM = 128


def dot(a, b):
    return jnp.dot(a, b, preferred_element_type=F32)


def dot_t(a, b):
    return lax.dot_general(a, b, (((1,), (1,)), ((), ())), preferred_element_type=F32)


def split_terms(twice):
    first = lax.broadcasted_iota(jnp.int32, twice.shape, 1) < twice.shape[1] // 2
    high = twice.astype(BF16).astype(F32)
    rest = twice - high
    middle = rest.astype(BF16).astype(F32)
    low = rest - middle
    return (jnp.where(first, high, middle).astype(BF16), jnp.where(first, low, 0.0).astype(BF16))


def diagonal(rows):
    shape = (rows, 128)
    return lax.broadcasted_iota(jnp.int32, shape, 0) == lax.broadcasted_iota(jnp.int32, shape, 1)


def encode(value, code, scale):
    top = jnp.maximum(jnp.max(jnp.abs(value), axis=1, keepdims=True), 1e-30)
    code[...] = jnp.round(value * (32760.0 / top)).astype(jnp.int32).astype(jnp.int16)
    row = jnp.sum(jnp.where(diagonal(code.shape[0]), top * (1.0 / 32760.0), 0.0), axis=0, keepdims=True)
    scale[...] = jnp.broadcast_to(row, (8, 128))


def decode(code, scale):
    rows = code.shape[0]
    row = jnp.broadcast_to(scale[0:1, :], (rows, 128))
    column = jnp.sum(jnp.where(diagonal(rows), row, 0.0), axis=1, keepdims=True)
    return code[...].astype(jnp.int32).astype(F32) * column


def kernel(x_in, w_in, down_in, up_in, dy_in, tiles_in, out, gx_out, gw,
           x_all, dy_all, w, tiles, mask, up_ext, down_ext, x_low, dy_low, x_t,
           p, p_sib, p_out, p_in, pz_out, pz_in, q, q_out, q_in, qz_out, qz_in, scale_out, scale_in, send, recv, local):
    r = lax.axis_index("row")
    c = lax.axis_index("col")
    core = lax.rem(r, 2)
    y, zl = r // 4, lax.rem(r // 2, 2)
    x, zh = c // 2, lax.rem(c, 2)
    other, zlo, zho = 1 - core, 1 - zl, 1 - zh
    yl, yr, yo = lax.rem(y + 3, 4), lax.rem(y + 1, 4), lax.rem(y + 2, 4)
    xl, xr, xo = lax.rem(x + 3, 4), lax.rem(x + 1, 4), lax.rem(x + 2, 4)
    sib, z_low, z_high = (r + 1 - 2 * core, c), (r + 2 - 4 * zl, c), (r, c + 1 - 2 * zh)
    y_left, y_right = (lax.rem(r + 12, 16), c), (lax.rem(r + 4, 16), c)
    x_left, x_right = (r, lax.rem(c + 6, 8)), (r, lax.rem(c + 2, 8))
    y_far, x_far = (lax.rem(r + 8, 16), c), (r, lax.rem(c + 4, 8))

    counter = [0]
    sends = []

    def ident():
        counter[0] += 1
        return counter[0] - 1

    scale_counter = [0]

    def scale_id():
        scale_counter[0] += 1
        return scale_counter[0] - 1

    def put(i, src, dst, device):
        copy = pltpu.make_async_remote_copy(
            src_ref=src, dst_ref=dst, send_sem=send.at[i], recv_sem=recv.at[i],
            device_id=device, device_id_type=MESH)
        copy.start()
        sends.append(copy)

    def relay(i, ref, device):
        put(i, ref, ref, device)

    def got(i, dst):
        pltpu.make_async_remote_copy(
            src_ref=dst, dst_ref=dst, send_sem=send.at[i], recv_sem=recv.at[i],
            device_id=sib, device_id_type=MESH).wait_recv()

    w_copy = pltpu.make_async_copy(w_in, w, local.at[0])
    w_copy.start()
    x_copy = pltpu.make_async_copy(x_in, x_all.at[x, zh], local.at[1])
    x_copy.start()
    dy_copy = pltpu.make_async_copy(dy_in, dy_all.at[y, zl, core], local.at[2])
    dy_copy.start()
    small = [pltpu.make_async_copy(tiles_in, tiles, local.at[3])]
    for part in range(3):
        rows = slice(64 * part, 64 * (part + 1))
        small.append(pltpu.make_async_copy(down_in, down_ext.at[rows], local.at[4 + part]))
        small.append(pltpu.make_async_copy(up_in, up_ext.at[rows], local.at[7 + part]))
    for copy in small:
        copy.start()

    barrier = pltpu.get_barrier_semaphore()
    partners = [sib, y_left, y_right, z_low, x_left, x_right, z_high]
    partners += [y_far] * P_DIRECT + [x_far] * Q_DIRECT
    for device in partners:
        pl.semaphore_signal(barrier, inc=1, device_id=device, device_id_type=MESH)
    pl.semaphore_wait(barrier, len(partners))

    def pair_of_ids():
        return [ident(), ident()]

    x0, x1r, x1l, x2r, x2l = (pair_of_ids() for _ in range(5))
    d0, d1r, d1l, d2r, d2l = (pair_of_ids() for _ in range(5))
    x3r, x3l, x4r, x4l, d3r, d3l, d4r, d4l = (ident() for _ in range(8))
    s = [ident() for _ in range(10)]
    for h in range(2):
        put(x0[h], x_in.at[h], x_all.at[x, zh, h], z_high)
        put(x1r[h], x_in.at[h], x_all.at[x, zh, h], x_right)
        put(x1l[1 - h], x_in.at[1 - h], x_all.at[x, zh, 1 - h], x_left)
        put(d1r[h], dy_in.at[h], dy_all.at[y, zl, core, h], y_right)
        put(d1l[1 - h], dy_in.at[1 - h], dy_all.at[y, zl, core, 1 - h], y_left)
    for h in range(2):
        put(d0[h], dy_in.at[h], dy_all.at[y, zl, core, h], z_low)
    put(s[0], dy_in, dy_all.at[y, zl, core], sib)

    small[0].wait()
    listed = tiles[...]
    number = lax.broadcasted_iota(jnp.int32, (8, listed.shape[1]), 0) * 26
    for tile in range(26):
        hit = jnp.where(jnp.broadcast_to(listed, number.shape) == number + tile, 1.0, 0.0)
        flag = jnp.sum(hit, axis=1, keepdims=True)
        mask[:, tile * 128:(tile + 1) * 128] = jnp.broadcast_to(flag, (8, 128))
    down_ext[192:, :] = jnp.zeros((64, 1024), BF16)
    up_ext[192:, :] = jnp.zeros((64, 3328), BF16)
    for copy in small[1:]:
        copy.wait()
    w_copy.wait()

    def masking(step, carry):
        at = pl.ds(pl.multiple_of(step * TILE, TILE), TILE)
        for block in range(8):
            rows = slice(block * 128, (block + 1) * 128)
            keep = mask[block:block + 1, at].astype(BF16)
            w[rows, at] = w[rows, at] * jnp.broadcast_to(keep, (128, TILE))
        return carry

    lax.fori_loop(0, 6, masking, 0)

    def span(chunk):
        return slice(chunk[0] * TILE, (chunk[0] + chunk[1]) * TILE)

    def ring_sum(direct, chunks, view, codes_out, codes_in, z_out, z_in, k, plane, order, left, right, opposite, z_device, finish):
        far, lower, upper = lax.rem(k + 2, 4), lax.rem(k + 3, 4), lax.rem(k + 1, 4)
        ids = [[(ident(), ident(), scale_id()) for _ in range(3)] for _ in range(4)]
        z_ids = [(ident(), ident(), scale_id()) for _ in range(2)]

        def where(n):
            return order[n // 2], span(chunks[n % 2])

        def post(key, value, code_out, code_in, device):
            data, scales, slot = key
            encode(value, code_out, scale_out.at[slot])
            put(data, code_out, code_in, device)
            put(scales, scale_out.at[slot], scale_in.at[slot], device)

        def take(key, code_in):
            data, scales, slot = key
            got(data, code_in)
            got(scales, scale_in.at[slot])
            return decode(code_in, scale_in.at[slot])

        def hop(n, i, value, device):
            h, at = where(n)
            post(ids[n][i], value, codes_out.at[i, h, :, at], codes_in.at[i, h, :, at], device)

        def came(n, i):
            h, at = where(n)
            return take(ids[n][i], codes_in.at[i, h, :, at])

        def first(n):
            h, at = where(n)
            hop(n, 0, view(h, far, at)[...], opposite if direct else (left, right)[n % 2])
            if direct or n % 2 == 0:
                hop(n, 2, view(h, upper, at)[...], right)
            if direct or n % 2 == 1:
                hop(n, 1, view(h, lower, at)[...], left)

        def second(n):
            if direct:
                return
            h, at = where(n)
            if n % 2 == 0:
                hop(n, 1, view(h, lower, at)[...] + came(n, 0), left)
            else:
                hop(n, 2, view(h, upper, at)[...] + came(n, 0), right)

        def third(n):
            h, at = where(n)
            total = view(h, k, at)
            value = total[...] + came(n, 1) + came(n, 2)
            total[...] = value + came(n, 0) if direct else value

        def across(j):
            at = span(chunks[j])
            post(z_ids[j], view(1 - plane, k, at)[...], z_out.at[:, at], z_in.at[:, at], z_device)

        def last(j):
            at = span(chunks[j])
            finish[:, at] = (view(plane, k, at)[...] + take(z_ids[j], z_in.at[:, at])).astype(BF16)

        return first, second, third, across, last

    def p_view(h, k, at):
        return p.at[h, k, core, :, at]

    def q_view(h, k, at):
        return q.at[h, k, :, at]

    p_first, p_second, p_third, p_across, p_last = ring_sum(
        P_DIRECT, P_CHUNKS, p_view, p_out, p_in, pz_out, pz_in, y, zl, (zh, zho), y_left, y_right, y_far, z_low, out)
    q_first, q_second, q_third, q_across, q_last = ring_sum(
        Q_DIRECT, G_CHUNKS, q_view, q_out, q_in, qz_out, qz_in, x, zh, (zl, zlo), x_left, x_right, x_far, z_high, gx_out)
    pair_ids = [ident() for _ in range(4)]

    def x_rows(h):
        return x_all[:, h].reshape(256, 1024)

    def p_low(h):
        parts = split_terms(dot_t(x_rows(h), down_ext[:128, :]))
        x_low[h, :, :128] = parts[0]
        x_low[h, :, 128:] = parts[1]

    def p_compute(n):
        h = (zh, zho)[n // 2]

        def step(i, carry):
            at = pl.ds(pl.multiple_of(i * TILE, TILE), TILE)
            value = dot(x_rows(h), w[:, at]) + dot(x_low[h], up_ext[:, at])
            p[h, :, :, :, at] = value.reshape(4, 2, 32, TILE)
            return carry

        begin, count = P_CHUNKS[n % 2]
        lax.fori_loop(begin, begin + count, step, 0, unroll=True)
        at = span(P_CHUNKS[n % 2])
        put(pair_ids[n], p.at[h, :, other, :, at], p_sib.at[h, :, :, at], sib)

    def p_pair(n):
        h, at = (zh, zho)[n // 2], span(P_CHUNKS[n % 2])
        got(pair_ids[n], p_sib.at[h, :, :, at])
        p[h, :, core, :, at] = p[h, :, core, :, at] + p_sib[h, :, :, at]
        p_first(n)

    def dy_rows(h):
        return dy_all[:, h].reshape(256, 3328)

    def q_low(h):
        parts = split_terms(dot_t(dy_rows(h), up_ext[:128, :]))
        dy_low[h, :, :128] = parts[0]
        dy_low[h, :, 128:] = parts[1]

    def q_compute(n):
        h = (zl, zlo)[n // 2]

        def step(i, carry):
            at = pl.ds(pl.multiple_of(i * TILE, TILE), TILE)
            value = dot_t(dy_rows(h), w[at, :]) + dot(dy_low[h], down_ext[:, at])
            q[h, :, :, at] = value.reshape(4, 64, TILE)
            return carry

        begin, count = G_CHUNKS[n % 2]
        lax.fori_loop(begin, begin + count, step, 0, unroll=True)
        q_first(n)

    def gw_compute(begin, end):
        def step(i, carry):
            at = pl.ds(pl.multiple_of(i * TILE, TILE), TILE)
            for half in range(2):
                rows = slice(half * 512, (half + 1) * 512)
                value = dot(x_t[rows, :], dy_all[:, :, :, :, :, at].reshape(512, TILE))
                for block in range(4):
                    keep = mask[half * 4 + block:half * 4 + block + 1, at] * (1.0 / math.sqrt(512))
                    gw[half * 512 + block * 128:half * 512 + (block + 1) * 128, at] = (
                        value[block * 128:(block + 1) * 128] * keep).astype(BF16)
            return carry

        lax.fori_loop(begin, end, step, 0, unroll=True)

    for h in range(2):
        got(x0[h], x_all.at[x, zho, h])
    for h in range(2):
        relay(x2r[h], x_all.at[x, zho, h], x_right)
        relay(x2l[1 - h], x_all.at[x, zho, 1 - h], x_left)
    got(x1r[0], x_all.at[xl, zh, 0])
    relay(x3r, x_all.at[xl, zh, 0], x_right)
    got(x1l[1], x_all.at[xr, zh, 1])
    relay(x3l, x_all.at[xr, zh, 1], x_left)
    got(d1r[0], dy_all.at[yl, zl, core, 0])
    relay(d3r, dy_all.at[yl, zl, core, 0], y_right)
    got(d1l[1], dy_all.at[yr, zl, core, 1])
    relay(d3l, dy_all.at[yr, zl, core, 1], y_left)
    lax.fori_loop(6, 13, masking, 0)
    got(d0[0], dy_all.at[y, zlo, core, 0])
    relay(d2r[0], dy_all.at[y, zlo, core, 0], y_right)
    got(d0[1], dy_all.at[y, zlo, core, 1])
    relay(d2l[1], dy_all.at[y, zlo, core, 1], y_left)
    relay(d2r[1], dy_all.at[y, zlo, core, 1], y_right)
    relay(d2l[0], dy_all.at[y, zlo, core, 0], y_left)
    relay(s[1], dy_all.at[y, zlo, core], sib)
    got(x2r[0], x_all.at[xl, zho, 0])
    relay(x4r, x_all.at[xl, zho, 0], x_right)
    got(x2l[1], x_all.at[xr, zho, 1])
    relay(x4l, x_all.at[xr, zho, 1], x_left)
    got(x1r[1], x_all.at[xl, zh, 1])
    got(x1l[0], x_all.at[xr, zh, 0])
    got(x3r, x_all.at[xo, zh, 0])
    got(x3l, x_all.at[xo, zh, 1])
    x_copy.wait()
    p_low(zh)
    p_compute(0)
    got(d1r[1], dy_all.at[yl, zl, core, 1])
    relay(s[2], dy_all.at[yl, zl, core], sib)
    got(d1l[0], dy_all.at[yr, zl, core, 0])
    relay(s[3], dy_all.at[yr, zl, core], sib)
    got(d2r[0], dy_all.at[yl, zlo, core, 0])
    relay(d4r, dy_all.at[yl, zlo, core, 0], y_right)
    got(d2l[1], dy_all.at[yr, zlo, core, 1])
    relay(d4l, dy_all.at[yr, zlo, core, 1], y_left)
    p_compute(1)
    p_pair(0)
    got(d3r, dy_all.at[yo, zl, core, 0])
    relay(s[6], dy_all.at[yo, zl, core, 0], sib)
    got(d3l, dy_all.at[yo, zl, core, 1])
    relay(s[7], dy_all.at[yo, zl, core, 1], sib)
    got(x2r[1], x_all.at[xl, zho, 1])
    got(x2l[0], x_all.at[xr, zho, 0])
    got(x4r, x_all.at[xo, zho, 0])
    got(x4l, x_all.at[xo, zho, 1])
    p_low(zho)
    p_compute(2)
    p_pair(1)
    p_compute(3)
    p_pair(2)
    got(d2r[1], dy_all.at[yl, zlo, core, 1])
    relay(s[4], dy_all.at[yl, zlo, core], sib)
    got(d2l[0], dy_all.at[yr, zlo, core, 0])
    relay(s[5], dy_all.at[yr, zlo, core], sib)
    p_pair(3)
    dy_copy.wait()
    got(s[0], dy_all.at[y, zl, other])
    got(s[2], dy_all.at[yl, zl, other])
    got(s[3], dy_all.at[yr, zl, other])
    got(s[6], dy_all.at[yo, zl, other, 0])
    got(s[7], dy_all.at[yo, zl, other, 1])
    q_low(zl)
    q_compute(0)
    p_second(0)
    q_compute(1)
    p_second(1)
    got(d4r, dy_all.at[yo, zlo, core, 0])
    relay(s[8], dy_all.at[yo, zlo, core, 0], sib)
    got(d4l, dy_all.at[yo, zlo, core, 1])
    relay(s[9], dy_all.at[yo, zlo, core, 1], sib)
    for quarter in range(4):
        cols = slice(quarter * 256, (quarter + 1) * 256)
        x_t[cols, :] = x_all[:, :, :, :, cols].reshape(512, 256).T
    p_second(2)
    got(s[1], dy_all.at[y, zlo, other])
    got(s[4], dy_all.at[yl, zlo, other])
    got(s[5], dy_all.at[yr, zlo, other])
    got(s[8], dy_all.at[yo, zlo, other, 0])
    got(s[9], dy_all.at[yo, zlo, other, 1])
    q_low(zlo)
    q_compute(2)
    q_second(0)
    p_second(3)
    q_compute(3)
    q_second(1)
    gw_compute(0, 3)
    q_second(2)
    p_third(0)
    gw_compute(3, 5)
    q_second(3)
    p_third(1)
    gw_compute(5, 7)
    q_third(0)
    q_third(1)
    p_third(2)
    p_across(0)
    gw_compute(7, 9)
    q_third(2)
    q_across(0)
    p_third(3)
    p_across(1)
    q_third(3)
    q_across(1)
    gw_compute(9, 13)
    p_last(0)
    q_last(0)
    p_last(1)
    q_last(1)
    for copy in sends:
        copy.wait_send()


def store(out, gx, gw, out_to, gx_to, gw_to, sems):
    pairs = [(gw.at[pl.ds(128 * i, 128)], gw_to.at[pl.ds(128 * i, 128)]) for i in range(8)]
    pairs += [(out, out_to), (gx, gx_to)]
    copies = [pltpu.make_async_copy(src, dst, sems.at[i]) for i, (src, dst) in enumerate(pairs)]
    for copy in copies:
        copy.start()
    for copy in copies:
        copy.wait()


def body(tokens, weight, down, up, grad_out, tile_list):
    anywhere = pl.BlockSpec(memory_space=pl.ANY)
    vmem = pl.BlockSpec(memory_space=pltpu.VMEM)
    scratch = [
        pltpu.VMEM((4, 2, 2, 32, 1024), BF16),
        pltpu.VMEM((4, 2, 2, 2, 16, 3328), BF16),
        pltpu.VMEM((1024, 3328), BF16),
        pltpu.VMEM((1, 156), jnp.int32),
        pltpu.VMEM((8, 3328), F32),
        pltpu.VMEM((256, 3328), BF16),
        pltpu.VMEM((256, 1024), BF16),
        pltpu.VMEM((2, 256, 256), BF16),
        pltpu.VMEM((2, 256, 256), BF16),
        pltpu.VMEM((1024, 512), BF16),
        pltpu.VMEM((2, 4, 2, 32, 3328), F32),
        pltpu.VMEM((2, 4, 32, 3328), F32),
        pltpu.VMEM((3, 2, 32, 3328), I16),
        pltpu.VMEM((3, 2, 32, 3328), I16),
        pltpu.VMEM((32, 3328), I16),
        pltpu.VMEM((32, 3328), I16),
        pltpu.VMEM((2, 4, 64, 1024), F32),
        pltpu.VMEM((3, 2, 64, 1024), I16),
        pltpu.VMEM((3, 2, 64, 1024), I16),
        pltpu.VMEM((64, 1024), I16),
        pltpu.VMEM((64, 1024), I16),
        pltpu.VMEM((28, 8, 128), F32),
        pltpu.VMEM((28, 8, 128), F32),
        pltpu.SemaphoreType.DMA((N_SEM,)),
        pltpu.SemaphoreType.DMA((N_SEM,)),
        pltpu.SemaphoreType.DMA((10,)),
    ]
    shapes = ((32, 3328), (64, 1024), (1024, 3328))
    results = pl.pallas_call(
        kernel,
        out_shape=tuple(pltpu.VMEM(shape, BF16) for shape in shapes),
        in_specs=[pl.BlockSpec(memory_space=pltpu.HBM)] * 6,
        out_specs=(vmem, vmem, vmem),
        scratch_shapes=scratch,
        compiler_params=pltpu.CompilerParams(
            collective_id=0, has_side_effects=True, vmem_limit_bytes=57 * 2**20),
        cost_estimate=pl.CostEstimate(flops=3 * 2 * 512 * 1024 * 3328, bytes_accessed=14 * 2**20, transcendentals=0),
    )(tokens.reshape(2, 32, 1024), weight, down.T, up, grad_out.reshape(2, 16, 3328), tile_list.reshape(1, -1))
    return pl.pallas_call(
        store,
        out_shape=tuple(jax.ShapeDtypeStruct(shape, BF16) for shape in shapes),
        in_specs=[vmem] * 3,
        out_specs=(anywhere,) * 3,
        scratch_shapes=[pltpu.SemaphoreType.DMA((10,))],
        compiler_params=pltpu.CompilerParams(vmem_limit_bytes=2**20),
        cost_estimate=pl.CostEstimate(flops=0, bytes_accessed=8 * 2**20, transcendentals=0),
    )(*results)


def solution(mesh):
    return jax.shard_map(
        body,
        mesh=mesh,
        in_specs=(
            P("col", "row"),
            P("row", "col"),
            P("row", None),
            P(None, "col"),
            P("row", "col"),
            P("row", "col", None),
        ),
        out_specs=(P("row", "col"), P("col", "row"), P("row", "col")),
        check_vma=False,
    )
```

time: 70.2 us -> 58.2 us (0.83)
  Pallas kernels: 69.5 us -> 57 us
    pallas_call x1, Pallas kernels: 66.5 us -> 54 us  [body(): pl.pallas_call(kernel, out_shape=tuple((pltpu.VMEM(shape, BF16) for shape...]
where the time goes in v3:
time: 58.2 us; the launch traced here: 57.6 us
  Pallas kernels  57 us (98%)
  between operations  0.64 us (1%)
    pallas_call x1, Pallas kernels, body(): pl.pallas_call(kernel, out_shape=tuple((pltpu.VMEM(shape, BF16) for shape...  54 us
    pallas_call x1, Pallas kernels, body(): pl.pallas_call(store, out_shape=tuple((jax.ShapeDtypeStruct(shape, BF16)...  2.98 us

profile of v3, /device:TPU:0, one launch (start us, length us, event | category | flops | bytes accessed | tf_op | source)
XLA Modules:
  0.0 57.6 jit_solution(8193817354339882189)
XLA Ops:
  0.6 54.0 %shard_map.85 = (bf16[32,3328]{1,0:T(8,128)(2,1)S(1)}, bf16[64,1024]{1,0:T(8,128)(2,1)S(1)}, bf16[1024,3328]{1,0:T(8,128)(2,1)S(1)}) custom-call(bf16[2,32,1024]{2,1,0:T(8,128)(2,1)} %bitcast.5, bf16[1024,3328]{1,0:T(8,128)(2,1)} %w_in.1, bf16[64,1024]{1,0:T(8,128)(2,1)} %bitcast.6, bf16[64,3328]{1,0:T(8,128)(2,1)} %up_in.1, bf16[2,16,3328]{2,1,0:T(8,128)(2,1)} %bitcast.4, ...), custom_call_target="tpu_custom_call" | custom-call | flops 10468982784 | bytes 14680064 | tf_op jit(solution)/shard_map/pallas_call | solution.py:461
  54.6 3.0 %shard_map.86 = (bf16[32,3328]{1,0:T(8,128)(2,1)}, bf16[64,1024]{1,0:T(8,128)(2,1)}, bf16[1024,3328]{1,0:T(8,128)(2,1)}) custom-call(bf16[32,3328]{1,0:T(8,128)(2,1)S(1)} %get-tuple-element.6.out, bf16[64,1024]{1,0:T(8,128)(2,1)S(1)} %get-tuple-element.7.gx, bf16[1024,3328]{1,0:T(8,128)(2,1)S(1)} %get-tuple-element.8.gw), custom_call_target="tpu_custom_call" | custom-call | bytes 8388608 | tf_op jit(solution)/shard_map/pallas_call | solution.py:471

commit v4 on v3

--- a/solution.py
+++ b/solution.py
@@ -313,6 +313,17 @@
     got(d1l[1], dy_all.at[yr, zl, core, 1])
     relay(d3l, dy_all.at[yr, zl, core, 1], y_left)
     lax.fori_loop(6, 13, masking, 0)
+    got(x1r[1], x_all.at[xl, zh, 1])
+    got(x1l[0], x_all.at[xr, zh, 0])
+    got(x3r, x_all.at[xo, zh, 0])
+    got(x3l, x_all.at[xo, zh, 1])
+    x_copy.wait()
+    p_low(zh)
+    p_compute(0)
+    got(x2r[0], x_all.at[xl, zho, 0])
+    relay(x4r, x_all.at[xl, zho, 0], x_right)
+    got(x2l[1], x_all.at[xr, zho, 1])
+    relay(x4l, x_all.at[xr, zho, 1], x_left)
     got(d0[0], dy_all.at[y, zlo, core, 0])
     relay(d2r[0], dy_all.at[y, zlo, core, 0], y_right)
     got(d0[1], dy_all.at[y, zlo, core, 1])
@@ -320,31 +331,18 @@
     relay(d2r[1], dy_all.at[y, zlo, core, 1], y_right)
     relay(d2l[0], dy_all.at[y, zlo, core, 0], y_left)
     relay(s[1], dy_all.at[y, zlo, core], sib)
-    got(x2r[0], x_all.at[xl, zho, 0])
-    relay(x4r, x_all.at[xl, zho, 0], x_right)
-    got(x2l[1], x_all.at[xr, zho, 1])
-    relay(x4l, x_all.at[xr, zho, 1], x_left)
-    got(x1r[1], x_all.at[xl, zh, 1])
-    got(x1l[0], x_all.at[xr, zh, 0])
-    got(x3r, x_all.at[xo, zh, 0])
-    got(x3l, x_all.at[xo, zh, 1])
-    x_copy.wait()
-    p_low(zh)
-    p_compute(0)
     got(d1r[1], dy_all.at[yl, zl, core, 1])
     relay(s[2], dy_all.at[yl, zl, core], sib)
     got(d1l[0], dy_all.at[yr, zl, core, 0])
     relay(s[3], dy_all.at[yr, zl, core], sib)
-    got(d2r[0], dy_all.at[yl, zlo, core, 0])
-    relay(d4r, dy_all.at[yl, zlo, core, 0], y_right)
-    got(d2l[1], dy_all.at[yr, zlo, core, 1])
-    relay(d4l, dy_all.at[yr, zlo, core, 1], y_left)
+    got(d3r, dy_all.at[yo, zl, core, 0])
+    relay(d4r, dy_all.at[yo, zl, core, 0], z_low)
+    got(d3l, dy_all.at[yo, zl, core, 1])
+    relay(d4l, dy_all.at[yo, zl, core, 1], z_low)
+    relay(s[6], dy_all.at[yo, zl, core, 0], sib)
+    relay(s[7], dy_all.at[yo, zl, core, 1], sib)
     p_compute(1)
     p_pair(0)
-    got(d3r, dy_all.at[yo, zl, core, 0])
-    relay(s[6], dy_all.at[yo, zl, core, 0], sib)
-    got(d3l, dy_all.at[yo, zl, core, 1])
-    relay(s[7], dy_all.at[yo, zl, core, 1], sib)
     got(x2r[1], x_all.at[xl, zho, 1])
     got(x2l[0], x_all.at[xr, zho, 0])
     got(x4r, x_all.at[xo, zho, 0])
@@ -354,8 +352,10 @@
     p_pair(1)
     p_compute(3)
     p_pair(2)
+    got(d2r[0], dy_all.at[yl, zlo, core, 0])
     got(d2r[1], dy_all.at[yl, zlo, core, 1])
     relay(s[4], dy_all.at[yl, zlo, core], sib)
+    got(d2l[1], dy_all.at[yr, zlo, core, 1])
     got(d2l[0], dy_all.at[yr, zlo, core, 0])
     relay(s[5], dy_all.at[yr, zlo, core], sib)
     p_pair(3)
@@ -389,28 +389,26 @@
     p_second(3)
     q_compute(3)
     q_second(1)
-    gw_compute(0, 3)
-    q_second(2)
+    gw_compute(0, 2)
     p_third(0)
-    gw_compute(3, 5)
-    q_second(3)
     p_third(1)
-    gw_compute(5, 7)
+    gw_compute(2, 4)
+    p_third(2)
+    p_across(0)
     q_third(0)
     q_third(1)
-    p_third(2)
-    p_across(0)
-    gw_compute(7, 9)
+    gw_compute(4, 5)
+    p_third(3)
+    p_across(1)
+    gw_compute(5, 6)
     q_third(2)
     q_across(0)
-    p_third(3)
-    p_across(1)
     q_third(3)
     q_across(1)
-    gw_compute(9, 13)
+    gw_compute(6, 13)
     p_last(0)
+    p_last(1)
     q_last(0)
-    p_last(1)
     q_last(1)
     for copy in sends:
         copy.wait_send()

time: 58.2 us -> 55.9 us (0.960)
  Pallas kernels: 57 us -> 54.9 us
    pallas_call x1, Pallas kernels: 54 us -> 51.9 us  [body(): pl.pallas_call(kernel, out_shape=tuple((pltpu.VMEM(shape, BF16) for shape...]
where the time goes in v4:
time: 55.9 us; the launch traced here: 55.6 us
  Pallas kernels  54.9 us (98%)
  between operations  0.64 us (1%)
    pallas_call x1, Pallas kernels, body(): pl.pallas_call(kernel, out_shape=tuple((pltpu.VMEM(shape, BF16) for shape...  51.9 us
    pallas_call x1, Pallas kernels, body(): pl.pallas_call(store, out_shape=tuple((jax.ShapeDtypeStruct(shape, BF16)...  2.98 us

profile of v4, /device:TPU:0, one launch (start us, length us, event | category | flops | bytes accessed | tf_op | source)
XLA Modules:
  0.0 55.6 jit_solution(4818716879639508138)
XLA Ops:
  0.6 51.9 %shard_map.85 = (bf16[32,3328]{1,0:T(8,128)(2,1)S(1)}, bf16[64,1024]{1,0:T(8,128)(2,1)S(1)}, bf16[1024,3328]{1,0:T(8,128)(2,1)S(1)}) custom-call(bf16[2,32,1024]{2,1,0:T(8,128)(2,1)} %bitcast.5, bf16[1024,3328]{1,0:T(8,128)(2,1)} %w_in.1, bf16[64,1024]{1,0:T(8,128)(2,1)} %bitcast.6, bf16[64,3328]{1,0:T(8,128)(2,1)} %up_in.1, bf16[2,16,3328]{2,1,0:T(8,128)(2,1)} %bitcast.4, ...), custom_call_target="tpu_custom_call" | custom-call | flops 10468982784 | bytes 14680064 | tf_op jit(solution)/shard_map/pallas_call | solution.py:459
  52.6 3.0 %shard_map.86 = (bf16[32,3328]{1,0:T(8,128)(2,1)}, bf16[64,1024]{1,0:T(8,128)(2,1)}, bf16[1024,3328]{1,0:T(8,128)(2,1)}) custom-call(bf16[32,3328]{1,0:T(8,128)(2,1)S(1)} %get-tuple-element.6.out, bf16[64,1024]{1,0:T(8,128)(2,1)S(1)} %get-tuple-element.7.gx, bf16[1024,3328]{1,0:T(8,128)(2,1)S(1)} %get-tuple-element.8.gw), custom_call_target="tpu_custom_call" | custom-call | bytes 8388608 | tf_op jit(solution)/shard_map/pallas_call | solution.py:469

commit v5 on v4

--- a/solution.py
+++ b/solution.py
@@ -328,12 +328,12 @@
     relay(d2r[0], dy_all.at[y, zlo, core, 0], y_right)
     got(d0[1], dy_all.at[y, zlo, core, 1])
     relay(d2l[1], dy_all.at[y, zlo, core, 1], y_left)
-    relay(d2r[1], dy_all.at[y, zlo, core, 1], y_right)
-    relay(d2l[0], dy_all.at[y, zlo, core, 0], y_left)
     relay(s[1], dy_all.at[y, zlo, core], sib)
     got(d1r[1], dy_all.at[yl, zl, core, 1])
+    relay(d2r[1], dy_all.at[yl, zl, core, 1], z_low)
     relay(s[2], dy_all.at[yl, zl, core], sib)
     got(d1l[0], dy_all.at[yr, zl, core, 0])
+    relay(d2l[0], dy_all.at[yr, zl, core, 0], z_low)
     relay(s[3], dy_all.at[yr, zl, core], sib)
     got(d3r, dy_all.at[yo, zl, core, 0])
     relay(d4r, dy_all.at[yo, zl, core, 0], z_low)
@@ -389,26 +389,24 @@
     p_second(3)
     q_compute(3)
     q_second(1)
+    p_third(0)
     gw_compute(0, 2)
-    p_third(0)
     p_third(1)
-    gw_compute(2, 4)
+    q_third(0)
     p_third(2)
     p_across(0)
-    q_third(0)
+    gw_compute(2, 4)
     q_third(1)
-    gw_compute(4, 5)
+    q_third(2)
+    q_across(0)
     p_third(3)
     p_across(1)
-    gw_compute(5, 6)
-    q_third(2)
-    q_across(0)
     q_third(3)
     q_across(1)
-    gw_compute(6, 13)
+    gw_compute(4, 13)
     p_last(0)
+    q_last(0)
     p_last(1)
-    q_last(0)
     q_last(1)
     for copy in sends:
         copy.wait_send()

time: 55.9 us -> 55.5 us (level)
  no operation moved by 1% of the time
where the time goes in v5:
time: 55.5 us; the launch traced here: 55.3 us
  Pallas kernels  54.7 us (99%)
  between operations  0.64 us (1%)
    pallas_call x1, Pallas kernels, body(): pl.pallas_call(kernel, out_shape=tuple((pltpu.VMEM(shape, BF16) for shape...  51.7 us
    pallas_call x1, Pallas kernels, body(): pl.pallas_call(store, out_shape=tuple((jax.ShapeDtypeStruct(shape, BF16)...  2.98 us

profile of v5, /device:TPU:0, one launch (start us, length us, event | category | flops | bytes accessed | tf_op | source)
XLA Modules:
  0.0 55.3 jit_solution(15583054278901945216)
XLA Ops:
  0.6 51.7 %shard_map.85 = (bf16[32,3328]{1,0:T(8,128)(2,1)S(1)}, bf16[64,1024]{1,0:T(8,128)(2,1)S(1)}, bf16[1024,3328]{1,0:T(8,128)(2,1)S(1)}) custom-call(bf16[2,32,1024]{2,1,0:T(8,128)(2,1)} %bitcast.5, bf16[1024,3328]{1,0:T(8,128)(2,1)} %w_in.1, bf16[64,1024]{1,0:T(8,128)(2,1)} %bitcast.6, bf16[64,3328]{1,0:T(8,128)(2,1)} %up_in.1, bf16[2,16,3328]{2,1,0:T(8,128)(2,1)} %bitcast.4, ...), custom_call_target="tpu_custom_call" | custom-call | flops 10468982784 | bytes 14680064 | tf_op jit(solution)/shard_map/pallas_call | solution.py:457
  52.3 3.0 %shard_map.86 = (bf16[32,3328]{1,0:T(8,128)(2,1)}, bf16[64,1024]{1,0:T(8,128)(2,1)}, bf16[1024,3328]{1,0:T(8,128)(2,1)}) custom-call(bf16[32,3328]{1,0:T(8,128)(2,1)S(1)} %get-tuple-element.6.out, bf16[64,1024]{1,0:T(8,128)(2,1)S(1)} %get-tuple-element.7.gx, bf16[1024,3328]{1,0:T(8,128)(2,1)S(1)} %get-tuple-element.8.gw), custom_call_target="tpu_custom_call" | custom-call | bytes 8388608 | tf_op jit(solution)/shard_map/pallas_call | solution.py:467
